TPU v7x, 32 devices: a whole 2x2x4 slice. The times are simulated.
32 devices in a mesh: seq: 8 (over y, x, core), dp: 4 (over z).
Axes of the slice: x: 2, y: 2, z: 4, core: 2. Of those that a mesh axis runs over, the one named last changes fastest.
Arguments:
- queries: bfloat16 [4, 4096, 1024], P('dp', 'seq'), may hold values from -6 to 6
- key_rows: bfloat16 [4, 4096, 1024], P('dp', 'seq'), may hold values from -6 to 6
- value_rows: bfloat16 [4, 4096, 1024], P('dp', 'seq'), may hold values from -6 to 6
- gate_rows: bfloat16 [4, 4096, 1024], P('dp', 'seq'), may hold values from -6 to 6
- cotangent: bfloat16 [4, 4096, 1024], P('dp', 'seq'), may hold values from -6 to 6
- far_blocks: int32 [4, 32, 4], P('dp'), may hold values from 0 to 31, as said below
- treated: int32 [4, 32], P('dp'), may hold values 0 or 1
- norm_gain: float32 [1024], replicated, may hold values from 0.1 to 1.9
- out_weight: bfloat16 [1024, 1024], replicated, may hold values from -0.1875 to 0.1875
Outputs:
- output: bfloat16 [4, 4096, 1024], P('dp', 'seq')
- grad_queries: bfloat16 [4, 4096, 1024], P('dp', 'seq')
- grad_keys: bfloat16 [4, 4096, 1024], P('dp', 'seq')
- grad_values: bfloat16 [4, 4096, 1024], P('dp', 'seq')
- grad_gate: bfloat16 [4, 4096, 1024], P('dp', 'seq')
- grad_weight: float32 [1024, 1024], P(('seq', 'dp'))
- grad_gain: float32 [1024], replicated
Inputs may be any that keep to these rules, and one draw needn't show every extreme that they name: `far_blocks`: every entry names a block of the same history that is held by another index of seq than its query block. Of the 16 entries of the query blocks held by index s of seq, 3 name blocks of index (s + o) mod 8 for o = 1 and o = 2, and 2 for each other o from 3 to 7; which entries these are, and which block of that index, are drawn.
All inputs are finite; a program needn't handle non-finite values. No bound on the sum of `treated` on one device may be relied on, other than what follows from the above.
Results may differ from a plain program's by a relative error of at most 0.0065.
Values may be sent and summed in bfloat16 or wider, within the bound.
A program may use at most 192 MiB of HBM per device.

v0:
```python
import jax
import jax.numpy as jnp
from jax import lax
from jax.sharding import PartitionSpec as P

HEADS = 8
HEAD_DIM = 128
BLK = 128
FAR = 4
epsilon = 1e-05


def from_behind(value, axis, by):
    peers = lax.axis_size(axis)
    pairs = [(i, i + by) for i in range(peers) if 0 <= i + by < peers]
    return lax.ppermute(value, axis, pairs)


def to_heads(rows):
    return rows.reshape(rows.shape[:-1] + (HEADS, rows.shape[-1] // HEADS))


def as_bf16(values):
    return values.astype(jnp.bfloat16)


def pair_scores(query_part, key_part):
    scores = jnp.einsum(
        "pqhd,pkhd->phqk",
        to_heads(query_part),
        to_heads(key_part),
        preferred_element_type=jnp.float32,
    )
    return scores * HEAD_DIM ** (-0.5)


def pair_forward(query_part, key_part, value_part, pair_mask):
    weights = as_bf16(jax.nn.silu(pair_scores(query_part, key_part)) * pair_mask[:, None])
    result = jnp.einsum(
        "phqk,pkhd->pqhd", weights, to_heads(value_part), preferred_element_type=jnp.float32
    )
    return result.reshape(query_part.shape)


def pair_backward(query_part, key_part, value_part, grad_part, pair_mask):
    scores = pair_scores(query_part, key_part)
    logistic = jax.nn.sigmoid(scores)
    weights = as_bf16(jax.nn.silu(scores) * pair_mask[:, None])
    grad_heads = to_heads(grad_part)
    grad_weights = jnp.einsum(
        "pqhd,pkhd->phqk", grad_heads, to_heads(value_part), preferred_element_type=jnp.float32
    )
    grad_value = jnp.einsum(
        "phqk,pqhd->pkhd", weights, grad_heads, preferred_element_type=jnp.float32
    )
    grad_scores = as_bf16(
        grad_weights
        * logistic
        * (1.0 + scores * (1.0 - logistic))
        * pair_mask[:, None]
        * HEAD_DIM ** (-0.5)
    )
    grad_query = jnp.einsum(
        "phqk,pkhd->pqhd", grad_scores, to_heads(key_part), preferred_element_type=jnp.float32
    )
    grad_key = jnp.einsum(
        "phqk,pqhd->pkhd", grad_scores, to_heads(query_part), preferred_element_type=jnp.float32
    )
    row_shape = query_part.shape
    return (
        grad_query.reshape(row_shape),
        grad_key.reshape(row_shape),
        grad_value.reshape(row_shape),
    )


def far_plan(far_all, my_index, seq_count, blocks, capacity):
    block_ids = far_all.reshape(seq_count, blocks * FAR)
    owners = block_ids // blocks
    local_ids = block_ids % blocks
    positions = jnp.arange(blocks * FAR)
    same_owner = owners[:, :, None] == owners[:, None, :]
    before = positions[None, :] < positions[:, None]
    slot_rank = jnp.sum(same_owner & before[None], axis=2)
    slot_ids = jnp.arange(capacity)
    send_hit = (owners[:, None, :] == my_index) & (slot_rank[:, None, :] == slot_ids[None, :, None])
    all_local = jnp.sum(jnp.where(send_hit, local_ids[:, None, :], 0), axis=2).reshape(-1)
    all_ok = jnp.any(send_hit, axis=2).reshape(-1)
    my_owners = lax.dynamic_index_in_dim(owners, my_index, 0, keepdims=False)
    my_ranks = lax.dynamic_index_in_dim(slot_rank, my_index, 0, keepdims=False)
    slot_count = seq_count * capacity
    read_at = my_owners * capacity + my_ranks
    back_hit = read_at[None, :] == jnp.arange(slot_count)[:, None]
    return (all_local, all_ok, read_at, back_hit)


def body(
    queries, key_rows, value_rows, gate_rows, cotangent, far_blocks, treated, norm_gain, out_weight
):
    width = queries.shape[2]
    blocks = queries.shape[1] // BLK
    seq_count = lax.axis_size("seq")
    my_index = lax.axis_index("seq")
    requests = blocks * FAR
    capacity = (requests + seq_count - 2) // (seq_count - 1)
    slot_count = seq_count * capacity
    query_blocks = queries[0].reshape(blocks, BLK, width)
    key_blocks = key_rows[0].reshape(blocks, BLK, width)
    value_blocks = value_rows[0].reshape(blocks, BLK, width)
    both_blocks = jnp.concatenate([key_blocks, value_blocks], axis=2)
    from_prev = from_behind(both_blocks[blocks - 1], "seq", 1)
    prev_both = jnp.concatenate([from_prev[None], both_blocks[:-1]], axis=0)
    prev_keys = prev_both[:, :, :width]
    prev_values = prev_both[:, :, width:]
    causal = jnp.tril(jnp.ones((BLK, BLK), jnp.float32))[None]
    all_ones = jnp.ones((1, BLK, BLK), jnp.float32)
    all_local, all_ok, read_at, back_hit = far_plan(
        far_blocks[0], my_index, seq_count, blocks, capacity
    )
    block_ids = lax.dynamic_slice_in_dim(far_blocks[0], my_index * blocks, blocks, 0).reshape(
        requests
    )
    far_mask = treated[0][block_ids].astype(jnp.float32)[:, None, None]
    far_queries = jnp.repeat(query_blocks, FAR, axis=0)
    back_matrix = back_hit.astype(jnp.bfloat16)
    local_onehot = ((all_local[None, :] == jnp.arange(blocks)[:, None]) & all_ok[None, :]).astype(
        jnp.bfloat16
    )
    diag_out = pair_forward(query_blocks, key_blocks, value_blocks, causal)
    prev_out = pair_forward(query_blocks, prev_keys, prev_values, all_ones)
    send_both = jnp.where(
        all_ok[:, None, None], both_blocks[all_local], jnp.zeros((), jnp.bfloat16)
    )
    got_both = lax.all_to_all(
        send_both.reshape(seq_count, capacity, BLK, 2 * width),
        "seq",
        split_axis=0,
        concat_axis=0,
        tiled=True,
    )
    received = got_both.reshape(slot_count, BLK, 2 * width)
    far_both = received[read_at]
    far_keys = far_both[:, :, :width]
    far_values = far_both[:, :, width:]
    far_terms = as_bf16(pair_forward(far_queries, far_keys, far_values, far_mask))
    far_sum = (
        lax.optimization_barrier(far_terms)
        .astype(jnp.float32)
        .reshape(blocks, FAR, BLK, width)
        .sum(axis=1)
    )
    attention = (diag_out + prev_out + far_sum).reshape(blocks * BLK, width)
    centered = attention - jnp.mean(attention, axis=1, keepdims=True)
    inv_std = lax.rsqrt(jnp.mean(centered * centered, axis=1, keepdims=True) + epsilon)
    normed = centered * inv_std
    gate_vals = gate_rows[0].astype(jnp.float32)
    mixed = as_bf16(normed * norm_gain * gate_vals)
    output = jnp.dot(mixed, out_weight, preferred_element_type=jnp.float32).astype(jnp.bfloat16)
    grad_in = cotangent[0]
    grad_mixed = lax.dot_general(
        grad_in, out_weight, (((1,), (1,)), ((), ())), preferred_element_type=jnp.float32
    )
    grad_weight = lax.psum_scatter(
        lax.dot_general(
            mixed, grad_in, (((0,), (0,)), ((), ())), preferred_element_type=jnp.float32
        ),
        ("seq", "dp"),
        scatter_dimension=0,
        tiled=True,
    )
    grad_gate = as_bf16(grad_mixed * normed * norm_gain)
    scaled = grad_mixed * gate_vals
    grad_gain = lax.psum(jnp.sum(scaled * normed, axis=0), ("seq", "dp"))
    grad_hat = scaled * norm_gain
    grad_attn = inv_std * (
        grad_hat
        - jnp.mean(grad_hat, axis=1, keepdims=True)
        - normed * jnp.mean(grad_hat * normed, axis=1, keepdims=True)
    )
    grad_blocks = as_bf16(grad_attn).reshape(blocks, BLK, width)
    dq_diag, dk_diag, dv_diag = pair_backward(
        query_blocks, key_blocks, value_blocks, grad_blocks, causal
    )
    dq_prev, dk_prev, dv_prev = pair_backward(
        query_blocks, prev_keys, prev_values, grad_blocks, all_ones
    )
    prev_terms = lax.optimization_barrier(as_bf16(jnp.concatenate([dk_prev, dv_prev], axis=2)))
    from_next = from_behind(prev_terms[0], "seq", -1)
    next_terms = jnp.concatenate([prev_terms[1:], from_next[None]], axis=0).astype(jnp.float32)
    far_grads = jnp.repeat(grad_blocks, FAR, axis=0)
    dq_far, dk_far, dv_far = pair_backward(far_queries, far_keys, far_values, far_grads, far_mask)
    query_terms = as_bf16(dq_far)
    back_terms = as_bf16(jnp.concatenate([dk_far, dv_far], axis=2))
    send_back = jnp.dot(
        back_matrix, back_terms.reshape(requests, -1), preferred_element_type=jnp.float32
    )
    send_back = as_bf16(send_back).reshape(slot_count, BLK, 2 * width)
    got_back = lax.all_to_all(
        send_back.reshape(seq_count, capacity, BLK, 2 * width),
        "seq",
        split_axis=0,
        concat_axis=0,
        tiled=True,
    )
    owned_terms = got_back.reshape(slot_count, BLK * 2 * width)
    far_query = (
        lax.optimization_barrier(query_terms)
        .astype(jnp.float32)
        .reshape(blocks, FAR, BLK, width)
        .sum(axis=1)
    )
    owned_sum = jnp.dot(
        local_onehot, lax.optimization_barrier(owned_terms), preferred_element_type=jnp.float32
    )
    owned_sum = owned_sum.reshape(blocks, BLK, 2 * width)
    rows = blocks * BLK
    grad_queries = as_bf16(dq_diag + dq_prev + far_query).reshape(1, rows, width)
    key_total = jnp.concatenate([dk_diag, dv_diag], axis=2) + next_terms + owned_sum
    grad_keys = as_bf16(key_total[:, :, :width]).reshape(1, rows, width)
    grad_values = as_bf16(key_total[:, :, width:]).reshape(1, rows, width)
    return (
        output[None],
        grad_queries,
        grad_keys,
        grad_values,
        grad_gate[None],
        grad_weight,
        grad_gain,
    )


def solution(mesh):
    in_specs = (
        P("dp", "seq", None),
        P("dp", "seq", None),
        P("dp", "seq", None),
        P("dp", "seq", None),
        P("dp", "seq", None),
        P("dp", None, None),
        P("dp", None),
        P(),
        P(),
    )
    out_specs = (
        P("dp", "seq", None),
        P("dp", "seq", None),
        P("dp", "seq", None),
        P("dp", "seq", None),
        P("dp", "seq", None),
        P(("seq", "dp"), None),
        P(),
    )
    return jax.shard_map(body, mesh=mesh, in_specs=in_specs, out_specs=out_specs, check_vma=False)
```

profile of v0, /device:TPU:0, one launch (start us, length us, event | category | flops | bytes accessed | tf_op | source)
XLA Modules:
  0.0 594.2 jit_solution(34854243904092478)
XLA Ops:
  12.2 7.5 %gather_fusion = bf16[24,128,2048]{2,1,0:T(8,128)(2,1)} fusion(bf16[4,128,2048]{2,1,0:T(8,128)(2,1)} %pad_maximum_fusion.1, s32[1024]{0:T(1024)S(1)} %pad_clamp_fusion.2), kind=kCustom, calls=%fused_computation | custom fusion | bytes 25165920 | tf_op jit(solution)/shard_map/gather | solution.py:132
  19.7 10.6 %broadcast_select_fusion = bf16[8,3,128,2048]{3,2,1,0:T(8,128)(2,1)} fusion(bf16[8,3,128,2048]{3,2,1,0:T(8,128)(2,1)} %bitcast.251, pred[8,3]{1,0:T(8,128)(4,1)S(1)} %copy.282), kind=kLoop, calls=%fused_computation.4 | loop fusion | flops 6291456 | bytes 25165848 | tf_op jit(solution)/shard_map/jit(_where)/select_n | solution.py:131
  30.3 5.5 all-to-all-start
  58.4 4.4 fusion.40
  73.0 102.6 %all-to-all-done = bf16[8,3,128,2048]{3,2,1,0:T(8,128)(2,1)} async-done(((bf16[8,3,128,2048]{3,2,1,0:T(8,128)(2,1)}), bf16[8,3,128,2048]{3,2,1,0:T(8,128)(2,1)}, u32[]{:S(2)}, u32[]{:S(2)}) %all-to-all-start) | async-done | bytes 12582944 | tf_op jit(solution)/shard_map/all_to_all | solution.py:134
  175.6 9.5 %gather_fusion.1 = bf16[16,128,2048]{2,1,0:T(8,128)(2,1)} fusion(bf16[24,128,2048]{2,1,0:T(8,128)(2,1)} %bitcast.11, s32[1024]{0:T(1024)S(1)} %pad_clamp_fusion.1), kind=kCustom, calls=%fused_computation.1 | custom fusion | bytes 16777280 | tf_op jit(solution)/shard_map/gather | solution.py:142
  185.1 6.1 %fusion.73 = (bf16[16,128,1024]{2,1,0:T(8,128)(2,1)}, bf16[16,128,1024]{2,1,0:T(8,128)(2,1)}) fusion(bf16[16,128,2048]{2,1,0:T(8,128)(2,1)} %gather_fusion.1), kind=kLoop, calls=%fused_computation.143 | loop fusion | bytes 16777216 | tf_op jit(solution)/shard_map/slice | solution.py:143
  191.1 6.4 %copy.285 = bf16[16,128,1024]{1,2,0:T(8,128)(2,1)} copy(bf16[16,128,1024]{2,1,0:T(8,128)(2,1)} %get-tuple-element.18) | data formatting | bytes 8388608 | tf_op jit(solution)/shard_map/slice | solution.py:143
  197.6 6.3 %copy.284 = bf16[16,128,1024]{1,2,0:T(8,128)(2,1)} copy(bf16[16,128,1024]{2,1,0:T(8,128)(2,1)} %get-tuple-element.19) | data formatting | bytes 8388608 | tf_op jit(solution)/shard_map/slice | solution.py:144
  206.3 5.6 fusion.4
  219.0 5.4 fusion.71
  227.5 4.6 fusion.31
  239.8 5.0 convolution_convert_fusion.1
  244.8 12.7 %fusion.9 = bf16[16,8,128,128]{2,3,1,0:T(8,128)(2,1)} fusion(f32[16,8,128,128]{3,2,1,0:T(8,128)} %get-tuple-element.29, f32[16]{0:T(128)S(1)} %convert_element_type.121, bf16[16,128,8,128]{1,3,2,0:T(8,128)(2,1)} %bitcast.258, bf16[16,128,8,128]{1,3,2,0:T(8,128)(2,1)} %bitcast.261), kind=kOutput, calls=%fused_computation.20 | convolution fusion | flops 562036736 | bytes 20971584 | tf_op jit(solution)/shard_map/pqhd,pkhd->phqk/dot_general | solution.py:50
  257.4 6.7 %copy.315 = bf16[16,128,1024]{2,1,0:T(8,128)(2,1)} copy(bf16[16,128,1024]{1,2,0:T(8,128)(2,1)} %bitcast.263) | data formatting | bytes 8388608 | tf_op jit(solution)/shard_map/reshape | solution.py:73
  264.1 8.4 %convolution_convert_fusion.2 = bf16[16,8,128,128]{2,3,1,0:T(8,128)(2,1)} fusion(bf16[16,8,128,128]{2,3,1,0:T(8,128)(2,1)} %fusion.9, bf16[16,128,8,128]{1,3,2,0:T(8,128)(2,1)} %bitcast.256), kind=kOutput, calls=%fused_computation.26 | convolution fusion | flops 538968064 | bytes 12582912 | tf_op jit(solution)/shard_map/phqk,pqhd->pkhd/dot_general | solution.py:66
  272.5 6.4 %copy.314 = bf16[16,128,1024]{2,1,0:T(8,128)(2,1)} copy(bf16[16,128,1024]{1,2,0:T(8,128)(2,1)} %bitcast.265) | data formatting | bytes 8388608 | tf_op jit(solution)/shard_map/reshape | solution.py:72
  279.0 8.3 %pad_maximum_fusion = bf16[16,128,2048]{2,1,0:T(8,128)(2,1)} fusion(bf16[16,128,1024]{2,1,0:T(8,128)(2,1)} %copy.315, bf16[16,128,1024]{2,1,0:T(8,128)(2,1)} %copy.314), kind=kLoop, calls=%fused_computation.5 | loop fusion | flops 16777216 | bytes 16777216 | tf_op jit(solution)/shard_map/concatenate | solution.py:193
  287.3 11.3 %copy.339 = bf16[2,8,128,2048]{3,1,2,0:T(8,128)(2,1)} copy(bf16[2,8,128,2048]{3,2,1,0:T(8,128)(2,1)} %bitcast.252) | data formatting | bytes 16777216
  298.6 11.4 %convolution_convert_fusion = bf16[24,262144]{1,0:T(8,128)(2,1)} fusion(bf16[16,262144]{1,0:T(8,128)(2,1)} %bitcast.249, s32[16]{0:T(128)S(1)} %bitcast.300), kind=kOutput, calls=%fused_computation.3 | convolution fusion | flops 207618432 | bytes 20971584 | tf_op jit(solution)/shard_map/dot_general | solution.py:194
  309.9 14.7 %copy.340 = bf16[3,8,128,2048]{3,2,1,0:T(8,128)(2,1)} copy(bf16[3,8,128,2048]{3,1,2,0:T(8,128)(2,1)} %bitcast.247) | data formatting | bytes 25165824
  324.6 17.8 %all-to-all-start.1 = ((bf16[8,3,128,2048]{3,2,1,0:T(8,128)(2,1)}), bf16[8,3,128,2048]{3,2,1,0:T(8,128)(2,1)}, u32[]{:S(2)}, u32[]{:S(2)}) async-start(bf16[8,3,128,2048]{3,2,1,0:T(8,128)(2,1)} %bitcast.250), calls=%async_computation.1 | async-start | bytes 25165824 | tf_op jit(solution)/shard_map/all_to_all | solution.py:198
  345.0 4.3 fusion.18
  351.6 4.9 fusion.34
  362.1 3.4 fusion.28
  386.1 4.7 convolution_convert_fusion.3
  395.8 147.2 %psum.7 = f32[1024]{0:T(1024)} all-reduce(f32[1024]{0:T(1024)S(1)} %get-tuple-element.7), channel_id=1, replica_groups=mesh['seq'=8,'dp'=4] {'seq','dp'}, use_global_device_ids=true, to_apply=%region_11.12 | all-reduce | flops 1024 | bytes 8192 | tf_op jit(solution)/shard_map/psum | solution.py:173
  552.9 11.7 %copy.341 = bf16[3,8,128,2048]{3,1,2,0:T(8,128)(2,1)S(1)} copy(bf16[3,8,128,2048]{3,2,1,0:T(8,128)(2,1)} %bitcast.95) | data formatting | bytes 25165824
  564.6 3.3 fusion.56
  567.8 4.5 copy.354
  572.3 5.4 copy.316
  577.7 4.6 fusion.11
  (149 shorter events, 108.5 us)
Async XLA Ops:
  7.2 43.2 %copy-start = (bf16[1024,1024]{1,0:T(8,128)(2,1)S(1)}, bf16[1024,1024]{1,0:T(8,128)(2,1)}, u32[]{:S(2)}) copy-start(bf16[1024,1024]{1,0:T(8,128)(2,1)} %param.17) | copy-start | bytes 6291460
  9.0 3.2 copy-start.30
  30.3 5.5 copy-start.11
  30.3 145.3 %all-to-all-start = ((bf16[8,3,128,2048]{3,2,1,0:T(8,128)(2,1)}), bf16[8,3,128,2048]{3,2,1,0:T(8,128)(2,1)}, u32[]{:S(2)}, u32[]{:S(2)}) async-start(bf16[8,3,128,2048]{3,2,1,0:T(8,128)(2,1)} %broadcast_select_fusion), calls=%async_computation | async-start | bytes 25165824 | tf_op jit(solution)/shard_map/all_to_all | solution.py:134
  35.8 5.0 copy-start.32
  37.6 25.2 %collective-permute-start = (bf16[128,2048]{1,0:T(8,128)(2,1)}, bf16[128,2048]{1,0:T(8,128)(2,1)}, u32[]{:S(2)}, u32[]{:S(2)}) collective-permute-start(bf16[128,2048]{1,0:T(8,128)(2,1)} %fusion.48), channel_id=1, source_target_pairs={{0,4},{4,8},{8,12},{12,16},{16,20},{20,24},{24,28},{1,5},{5,9},{9,... | collective-permute-start | bytes 1572872 | tf_op jit(solution)/shard_map/ppermute | solution.py:16
  45.3 2.8 copy-start.14
  48.2 2.2 copy-start.28
  50.4 2.6 copy-start.1
  58.4 4.4 copy-start.19
  203.8 2.5 copy-start.9
  206.0 5.9 copy-start.7
  206.3 5.6 copy-start.10
  212.0 2.0 copy-start.5
  224.6 2.9 copy-start.29
  227.5 4.6 copy-start.4
  227.5 4.6 copy-start.12
  237.3 2.5 copy-start.6
  239.4 5.3 copy-start.8
  324.6 228.2 %all-to-all-start.1 = ((bf16[8,3,128,2048]{3,2,1,0:T(8,128)(2,1)}), bf16[8,3,128,2048]{3,2,1,0:T(8,128)(2,1)}, u32[]{:S(2)}, u32[]{:S(2)}) async-start(bf16[8,3,128,2048]{3,2,1,0:T(8,128)(2,1)} %bitcast.250), calls=%async_computation.1 | async-start | bytes 25165824 | tf_op jit(solution)/shard_map/all_to_all | solution.py:198
  342.4 244.6 %reduce-scatter.2.cloned.1.call-start = ((), (), s32[]{:S(2)}) async-start(), calls=%async_computation.3 | async-start | bytes 4325376 | tf_op jit(solution)/shard_map/reduce_scatter | solution.py:163
  365.5 1.6 copy-start.24
  365.5 1.9 copy-start.26
  368.3 2.3 copy-start.22
  368.3 2.6 copy-start.25
  384.6 193.1 %collective-permute-start.1 = (bf16[128,2048]{0,1:T(8,128)(2,1)}, bf16[128,2048]{0,1:T(8,128)(2,1)}, u32[]{:S(2)}, u32[]{:S(2)}) collective-permute-start(bf16[128,2048]{0,1:T(8,128)(2,1)} %slice_bitcast_fusion), channel_id=1, source_target_pairs={{4,0},{8,4},{12,8},{16,12},{20,16},{24,20},{28,24},{5,1},{9,5},{13... | collective-permute-start | bytes 1572872 | tf_op jit(solution)/shard_map/ppermute | solution.py:16
  543.0 3.1 copy-start.17
  543.0 3.1 copy-start.18
  546.1 2.0 copy-start.3
  546.1 2.2 copy-start.13
  548.4 2.3 copy-start.23
  548.4 2.3 copy-start.27
  (6 other events, 7.3 us)
Sparse Core Ops, SparseCore 0:
  356.6 152.8 reduce-scatter.1
where the time goes:
time: 606 us; the launch traced here: 594 us
  local copies, waits for them, and re-layouts  159 us (26%)
  blocking collectives  147 us (24%)
  waiting for transfers between devices  103 us (17%)
  matrix products  89.9 us (15%)
  other arithmetic  52.6 us (9%)
  starting transfers between devices  27.9 us (5%)
  between operations  14.8 us (2%)
    psum x1, blocking collectives, body(): grad_gain = lax.psum(jnp.sum(scaled * normed, axis=0), ('seq', 'dp'))  147 us
    all_to_all x1, waiting for transfers between devices, body(): lax.all_to_all(send_both.reshape(seq_count, capacity, BLK, 2 * width), 's...  103 us
    unnamed x75, local copies, waits for them, and re-layouts  57.6 us
    all_to_all x1, starting transfers between devices, body(): lax.all_to_all(send_back.reshape(seq_count, capacity, BLK, 2 * width), 's...  17.8 us
    dot_general x3, matrix products, pair_backward(): jnp.einsum('pqhd,pkhd->phqk', grad_heads, to_heads(value_part), preferred...  17.5 us
    slice x2, local copies, waits for them, and re-layouts, body(): far_keys = far_both[:, :, :width]  12.5 us
  transfers between devices with their start and end apart: 5, of which 1 were waited for; matrix products, arithmetic and copies ran while one was open for 21% of the time, Pallas kernels for 0%

commit v1 on v0

--- a/solution.py
+++ b/solution.py
@@ -8,6 +8,21 @@
 BLK = 128
 FAR = 4
 epsilon = 1e-05
+
+
+def pair_body_for(unit, which_dim, w_in):
+    main, reached = (unit.shape[:which_dim], unit.shape[which_dim + 1 :])
+    e_now = jnp.moveaxis(unit.reshape(*main, w_in, -1, *reached), which_dim, 0)
+    return e_now
+
+
+def tokens_attach(load, ndim_at):
+    load = jnp.moveaxis(load, 0, ndim_at)
+    item_now = load.shape
+    b_next = load.reshape(
+        *item_now[:ndim_at], item_now[ndim_at] * item_now[ndim_at + 1], *item_now[ndim_at + 2 :]
+    )
+    return b_next
 
 
 def from_behind(value, axis, by):
@@ -195,13 +210,25 @@
         back_matrix, back_terms.reshape(requests, -1), preferred_element_type=jnp.float32
     )
     send_back = as_bf16(send_back).reshape(slot_count, BLK, 2 * width)
-    got_back = lax.all_to_all(
-        send_back.reshape(seq_count, capacity, BLK, 2 * width),
-        "seq",
-        split_axis=0,
-        concat_axis=0,
-        tiled=True,
-    )
+
+    def store_forms_for(inner_x, mesh_ax, sheet, frame_in):
+        x_next, even = (lax.axis_size(mesh_ax), lax.axis_index(mesh_ax))
+        reply = pair_body_for(inner_x, sheet, x_next)
+        pile = [reply[even]]
+        for idx in range(1, x_next):
+            state_next = reply[(even + idx) % x_next]
+            pile.append(
+                lax.ppermute(
+                    state_next,
+                    axis_name=mesh_ax,
+                    perm=[(m, (m + idx) % x_next) for m in range(x_next)],
+                )
+            )
+        reply = jnp.stack(pile)[(even - jnp.arange(x_next)) % x_next]
+        piece_now = tokens_attach(reply, frame_in)
+        return piece_now
+
+    got_back = store_forms_for(send_back.reshape(seq_count, capacity, BLK, 2 * width), "seq", 0, 0)
     owned_terms = got_back.reshape(slot_count, BLK * 2 * width)
     far_query = (
         lax.optimization_barrier(query_terms)

time: 606 us -> 706 us (1.17)
  the two profiles are of different devices: /device:TPU:0 before, /device:TPU:3 now
where the time goes in v1:
time: 706 us; the launch traced here: 695 us
  waiting for transfers between devices  199 us (28%)
  local copies, waits for them, and re-layouts  184 us (26%)
  blocking collectives  132 us (19%)
  matrix products  92.1 us (13%)
  other arithmetic  51.7 us (7%)
  starting transfers between devices  21.7 us (3%)
  between operations  14.7 us (2%)
    psum x1, blocking collectives, body(): grad_gain = lax.psum(jnp.sum(scaled * normed, axis=0), ('seq', 'dp'))  132 us
    ppermute x2, waiting for transfers between devices, from_behind(): return lax.ppermute(value, axis, pairs)  110 us
    ppermute x7, waiting for transfers between devices, store_forms_for(): lax.ppermute(state_next, axis_name=mesh_ax, perm=[(m, (m + idx) % x_next)...  89 us
    unnamed x103, local copies, waits for them, and re-layouts  63.5 us
    dot_general x3, matrix products, pair_backward(): jnp.einsum('pqhd,pkhd->phqk', grad_heads, to_heads(value_part), preferred...  19.5 us
  transfers between devices with their start and end apart: 11, of which 3 were waited for; matrix products, arithmetic and copies ran while one was open for 20% of the time, Pallas kernels for 0%

profile of v1, /device:TPU:3, one launch (start us, length us, event | category | flops | bytes accessed | tf_op | source)
XLA Modules:
  0.0 694.7 jit_solution(7742643810599705089)
XLA Ops:
  13.1 7.5 %gather_fusion = bf16[24,128,2048]{2,1,0:T(8,128)(2,1)} fusion(bf16[4,128,2048]{2,1,0:T(8,128)(2,1)} %pad_maximum_fusion.1, s32[1024]{0:T(1024)S(1)} %get-tuple-element.40), kind=kCustom, calls=%fused_computation | custom fusion | bytes 25165920 | tf_op jit(solution)/shard_map/gather | solution.py:147
  20.6 10.7 %broadcast_select_fusion = bf16[8,3,128,2048]{3,2,1,0:T(8,128)(2,1)} fusion(bf16[8,3,128,2048]{3,2,1,0:T(8,128)(2,1)} %bitcast.283, pred[8,3]{1,0:T(8,128)(4,1)S(1)} %copy.282), kind=kLoop, calls=%fused_computation.5 | loop fusion | flops 6291456 | bytes 25165848 | tf_op jit(solution)/shard_map/jit(_where)/select_n | solution.py:146
  31.3 5.5 all-to-all-start
  63.8 4.4 fusion.40
  68.2 109.8 %collective-permute-done = bf16[128,2048]{1,0:T(8,128)(2,1)} collective-permute-done((bf16[128,2048]{1,0:T(8,128)(2,1)}, bf16[128,2048]{1,0:T(8,128)(2,1)}, u32[]{:S(2)}, u32[]{:S(2)}) %collective-permute-start) | collective-permute-done | bytes 524320 | tf_op jit(solution)/shard_map/ppermute | solution.py:31
  188.2 9.3 %gather_fusion.1 = bf16[16,128,2048]{2,1,0:T(8,128)(2,1)} fusion(bf16[24,128,2048]{2,1,0:T(8,128)(2,1)} %bitcast.11, s32[1024]{0:T(1024)S(1)} %pad_clamp_fusion.2), kind=kCustom, calls=%fused_computation.1 | custom fusion | bytes 16777280 | tf_op jit(solution)/shard_map/gather | solution.py:157
  197.5 6.1 fusion.75
  203.7 6.4 copy.285
  210.0 6.4 copy.284
  218.9 5.5 fusion.4
  231.9 5.4 fusion.73
  240.4 4.6 fusion.31
  251.6 4.5 fusion.28
  265.3 5.0 convolution_convert_fusion.1
  270.3 12.7 %fusion.9 = bf16[16,8,128,128]{2,3,1,0:T(8,128)(2,1)} fusion(f32[16,8,128,128]{3,2,1,0:T(8,128)} %get-tuple-element.37, f32[16]{0:T(128)S(1)} %convert_element_type.121, bf16[16,128,8,128]{1,3,2,0:T(8,128)(2,1)} %bitcast.291, bf16[16,128,8,128]{1,3,2,0:T(8,128)(2,1)} %bitcast.294), kind=kOutput, calls=%fused_computation.21 | convolution fusion | flops 562036736 | bytes 20971584 | tf_op jit(solution)/shard_map/pqhd,pkhd->phqk/dot_general | solution.py:65
  283.0 8.6 %convolution_convert_fusion.2 = bf16[16,8,128,128]{2,3,1,0:T(8,128)(2,1)} fusion(bf16[16,8,128,128]{2,3,1,0:T(8,128)(2,1)} %fusion.9, bf16[16,128,8,128]{1,3,2,0:T(8,128)(2,1)} %bitcast.289), kind=kOutput, calls=%fused_computation.27 | convolution fusion | flops 538968064 | bytes 12582912 | tf_op jit(solution)/shard_map/phqk,pqhd->pkhd/dot_general | solution.py:81
  310.9 6.4 copy.315
  317.2 4.5 convert_reduce_fusion
  324.7 6.8 copy.314
  331.4 8.2 %pad_maximum_fusion = bf16[16,128,2048]{2,1,0:T(8,128)(2,1)} fusion(bf16[16,128,1024]{2,1,0:T(8,128)(2,1)} %copy.315, bf16[16,128,1024]{2,1,0:T(8,128)(2,1)} %copy.314), kind=kLoop, calls=%fused_computation.6 | loop fusion | flops 16777216 | bytes 16777216 | tf_op jit(solution)/shard_map/concatenate | solution.py:208
  339.7 11.4 %copy.339 = bf16[2,8,128,2048]{3,1,2,0:T(8,128)(2,1)} copy(bf16[2,8,128,2048]{3,2,1,0:T(8,128)(2,1)} %bitcast.285) | data formatting | bytes 16777216
  354.4 11.3 %convolution_convert_fusion = bf16[24,262144]{1,0:T(8,128)(2,1)} fusion(bf16[16,262144]{1,0:T(8,128)(2,1)} %bitcast.281, s32[16]{0:T(128)S(1)} %bitcast.334), kind=kOutput, calls=%fused_computation.4 | convolution fusion | flops 207618432 | bytes 20971584 | tf_op jit(solution)/shard_map/dot_general | solution.py:209
  365.6 11.7 %copy.340 = bf16[3,8,128,2048]{3,2,1,0:T(8,128)(2,1)S(1)} copy(bf16[3,8,128,2048]{3,1,2,0:T(8,128)(2,1)} %bitcast.279) | data formatting | bytes 25165824
  377.3 5.6 dynamic-slice_bitcast_fusion
  397.9 131.7 %psum.7 = f32[1024]{0:T(1024)} all-reduce(f32[1024]{0:T(1024)S(1)} %get-tuple-element.7), channel_id=1, replica_groups=mesh['seq'=8,'dp'=4] {'seq','dp'}, use_global_device_ids=true, to_apply=%region_11.12 | all-reduce | flops 1024 | bytes 8192 | tf_op jit(solution)/shard_map/psum | solution.py:188
  546.9 71.0 %collective-permute-done.5 = bf16[1,3,128,2048]{3,2,1,0:T(8,128)(2,1)S(1)} collective-permute-done((bf16[1,3,128,2048]{3,2,1,0:T(8,128)(2,1)S(1)}, bf16[1,3,128,2048]{3,2,1,0:T(8,128)(2,1)S(1)}, u32[]{:S(2)}, u32[]{:S(2)}) %collective-permute-start.5) | collective-permute-done | bytes 1572896 | tf_op jit(solution)/shard_map/ppermute | solution.py:221
  619.2 18.0 %collective-permute-done.6 = bf16[1,3,128,2048]{3,2,1,0:T(8,128)(2,1)S(1)} collective-permute-done((bf16[1,3,128,2048]{3,2,1,0:T(8,128)(2,1)S(1)}, bf16[1,3,128,2048]{3,2,1,0:T(8,128)(2,1)S(1)}, u32[]{:S(2)}, u32[]{:S(2)}) %collective-permute-start.6) | collective-permute-done | bytes 1572896 | tf_op jit(solution)/shard_map/ppermute | solution.py:221
  642.6 11.1 %gather_fusion.3 = bf16[8,3,128,2048]{3,2,1,0:T(8,128)(2,1)} fusion(bf16[8,3,128,2048]{3,2,1,0:T(8,128)(2,1)} %bitcast.309, s32[1024]{0:T(1024)} %pad_clamp_fusion), kind=kCustom, calls=%fused_computation.3 | custom fusion | bytes 25165856 | tf_op jit(solution)/shard_map/gather | solution.py:227
  653.7 11.7 %copy.341 = bf16[3,8,128,2048]{3,1,2,0:T(8,128)(2,1)S(1)} copy(bf16[3,8,128,2048]{3,2,1,0:T(8,128)(2,1)} %bitcast.284) | data formatting | bytes 25165824
  668.6 4.4 copy.354
  673.1 5.4 copy.316
  678.5 4.6 fusion.11
  (194 shorter events, 144.0 us)
Async XLA Ops:
  7.2 44.8 %copy-start = (bf16[1024,1024]{1,0:T(8,128)(2,1)S(1)}, bf16[1024,1024]{1,0:T(8,128)(2,1)}, u32[]{:S(2)}) copy-start(bf16[1024,1024]{1,0:T(8,128)(2,1)} %param.17) | copy-start | bytes 6291460
  31.3 5.5 copy-start.14
  31.3 156.9 %all-to-all-start = ((bf16[8,3,128,2048]{3,2,1,0:T(8,128)(2,1)}), bf16[8,3,128,2048]{3,2,1,0:T(8,128)(2,1)}, u32[]{:S(2)}, u32[]{:S(2)}) async-start(bf16[8,3,128,2048]{3,2,1,0:T(8,128)(2,1)} %broadcast_select_fusion), calls=%async_computation | async-start | bytes 25165824 | tf_op jit(solution)/shard_map/all_to_all | solution.py:149
  36.8 650.9 %reduce-scatter.2.cloned.1.call-start = ((), (), s32[]{:S(2)}) async-start(), calls=%async_computation.2 | async-start | bytes 4325376 | tf_op jit(solution)/shard_map/reduce_scatter | solution.py:178
  38.6 139.4 %collective-permute-start = (bf16[128,2048]{1,0:T(8,128)(2,1)}, bf16[128,2048]{1,0:T(8,128)(2,1)}, u32[]{:S(2)}, u32[]{:S(2)}) collective-permute-start(bf16[128,2048]{1,0:T(8,128)(2,1)} %fusion.48), channel_id=1, source_target_pairs={{0,4},{4,8},{8,12},{12,16},{16,20},{20,24},{24,28},{1,5},{5,9},{9,... | collective-permute-start | bytes 1572872 | tf_op jit(solution)/shard_map/ppermute | solution.py:31
  63.8 114.2 %copy-start.25 = (bf16[3,128,2048]{2,1,0:T(8,128)(2,1)S(1)}, bf16[3,128,2048]{2,1,0:T(8,128)(2,1)}, u32[]{:S(2)}) copy-start(bf16[3,128,2048]{2,1,0:T(8,128)(2,1)} %fusion.29) | copy-start | bytes 4718596
  218.6 5.9 copy-start.9
  218.9 5.6 copy-start.13
  240.4 4.6 copy-start.2
  240.4 4.6 copy-start.15
  251.6 4.5 copy-start.31
  251.6 4.5 copy-start.35
  265.0 5.4 copy-start.10
  283.0 8.6 %copy-start.8 = (bf16[16,8,128,128]{2,3,1,0:T(8,128)(2,1)S(1)}, bf16[16,8,128,128]{2,3,1,0:T(8,128)(2,1)}, u32[]{:S(2)}) copy-start(bf16[16,8,128,128]{2,3,1,0:T(8,128)(2,1)} %fusion.9) | copy-start | bytes 12582916
  283.0 8.6 %copy-start.12 = (bf16[16,128,1024]{1,2,0:T(8,128)(2,1)S(1)}, bf16[16,128,1024]{1,2,0:T(8,128)(2,1)}, u32[]{:S(2)}) copy-start(bf16[16,128,1024]{1,2,0:T(8,128)(2,1)} %copy.285) | copy-start | bytes 12582916
  339.6 11.4 %copy-start.26 = (bf16[4,128,1024]{2,1,0:T(8,128)(2,1)S(1)}, bf16[4,128,1024]{2,1,0:T(8,128)(2,1)}, u32[]{:S(2)}) copy-start(bf16[4,128,1024]{2,1,0:T(8,128)(2,1)} %copy.320) | copy-start | bytes 3145732
  339.6 11.4 %copy-start.40 = (bf16[1,512,1024]{2,1,0:T(8,128)(2,1)S(1)}, bf16[1,512,1024]{2,1,0:T(8,128)(2,1)}, u32[]{:S(2)}) copy-start(bf16[1,512,1024]{2,1,0:T(8,128)(2,1)} %param.13) | copy-start | bytes 3145732
  377.3 9.9 %copy-start.20 = (bf16[4,128,2048]{1,2,0:T(8,128)(2,1)S(1)}, bf16[4,128,2048]{1,2,0:T(8,128)(2,1)}, u32[]{:S(2)}) copy-start(bf16[4,128,2048]{1,2,0:T(8,128)(2,1)} %pad_maximum_fusion.2) | copy-start | bytes 6291460
  377.3 10.7 %copy-start.4 = (f32[512,1024]{1,0:T(8,128)S(1)}, f32[512,1024]{1,0:T(8,128)}, u32[]{:S(2)}) copy-start(f32[512,1024]{1,0:T(8,128)} %copy-done.3) | copy-start | bytes 6291460
  377.3 10.7 %copy-start.16 = (bf16[1,512,1024]{2,1,0:T(8,128)(2,1)S(1)}, bf16[1,512,1024]{2,1,0:T(8,128)(2,1)}, u32[]{:S(2)}) copy-start(bf16[1,512,1024]{2,1,0:T(8,128)(2,1)} %param.12) | copy-start | bytes 3145732
  383.0 160.3 %collective-permute-start.4 = (bf16[1,3,128,2048]{3,2,1,0:T(8,128)(2,1)}, bf16[1,3,128,2048]{3,2,1,0:T(8,128)(2,1)}, u32[]{:S(2)}, u32[]{:S(2)}) collective-permute-start(bf16[1,3,128,2048]{3,2,1,0:T(8,128)(2,1)} %get-tuple-element.22), channel_id=1, source_target_pairs={{0,12},{4,16},{8,20},{12,24},{16,28},{20,0},{24,4},{28,8},{1,13},{... | collective-permute-start | bytes 4718600 | tf_op jit(solution)/shard_map/ppermute | solution.py:221
  385.7 152.0 %collective-permute-start.3 = (bf16[1,3,128,2048]{3,2,1,0:T(8,128)(2,1)}, bf16[1,3,128,2048]{3,2,1,0:T(8,128)(2,1)}, u32[]{:S(2)}, u32[]{:S(2)}) collective-permute-start(bf16[1,3,128,2048]{3,2,1,0:T(8,128)(2,1)} %get-tuple-element.23), channel_id=1, source_target_pairs={{0,8},{4,12},{8,16},{12,20},{16,24},{20,28},{24,0},{28,4},{1,9},{5... | collective-permute-start | bytes 4718600 | tf_op jit(solution)/shard_map/ppermute | solution.py:221
  385.7 147.9 %collective-permute-start.2 = (bf16[1,3,128,2048]{3,2,1,0:T(8,128)(2,1)}, bf16[1,3,128,2048]{3,2,1,0:T(8,128)(2,1)}, u32[]{:S(2)}, u32[]{:S(2)}) collective-permute-start(bf16[1,3,128,2048]{3,2,1,0:T(8,128)(2,1)} %get-tuple-element.24), channel_id=1, source_target_pairs={{0,4},{4,8},{8,12},{12,16},{16,20},{20,24},{24,28},{28,0},{1,5},{5... | collective-permute-start | bytes 4718600 | tf_op jit(solution)/shard_map/ppermute | solution.py:221
  393.3 136.3 %copy-start.36 = (bf16[4,128,8,128]{1,3,2,0:T(8,128)(2,1)S(1)}, bf16[4,128,8,128]{1,3,2,0:T(8,128)(2,1)}, u32[]{:S(2)}) copy-start(bf16[4,128,8,128]{1,3,2,0:T(8,128)(2,1)} %copy.307) | copy-start | bytes 3145732
  394.6 283.9 %collective-permute-start.1 = (bf16[128,2048]{0,1:T(8,128)(2,1)}, bf16[128,2048]{0,1:T(8,128)(2,1)}, u32[]{:S(2)}, u32[]{:S(2)}) collective-permute-start(bf16[128,2048]{0,1:T(8,128)(2,1)} %slice_bitcast_fusion), channel_id=1, source_target_pairs={{4,0},{8,4},{12,8},{16,12},{20,16},{24,20},{28,24},{5,1},{9,5},{13... | collective-permute-start | bytes 1572872 | tf_op jit(solution)/shard_map/ppermute | solution.py:31
  396.5 243.3 %collective-permute-start.8 = (bf16[1,3,128,2048]{3,2,1,0:T(8,128)(2,1)}, bf16[1,3,128,2048]{3,2,1,0:T(8,128)(2,1)}, u32[]{:S(2)}, u32[]{:S(2)}) collective-permute-start(bf16[1,3,128,2048]{3,2,1,0:T(8,128)(2,1)} %get-tuple-element.18), channel_id=1, source_target_pairs={{0,28},{4,0},{8,4},{12,8},{16,12},{20,16},{24,20},{28,24},{1,29},{... | collective-permute-start | bytes 4718600 | tf_op jit(solution)/shard_map/ppermute | solution.py:221
  533.6 84.4 %collective-permute-start.5 = (bf16[1,3,128,2048]{3,2,1,0:T(8,128)(2,1)S(1)}, bf16[1,3,128,2048]{3,2,1,0:T(8,128)(2,1)S(1)}, u32[]{:S(2)}, u32[]{:S(2)}) collective-permute-start(bf16[1,3,128,2048]{3,2,1,0:T(8,128)(2,1)S(1)} %copy-done.34), channel_id=1, source_target_pairs={{0,16},{4,20},{8,24},{12,28},{16,0},{20,4},{24,8},{28,12},{1,17},{... | collective-permute-start | bytes 4718600 | tf_op jit(solution)/shard_map/ppermute | solution.py:221
  537.6 5.6 copy-start.32
  537.6 99.6 %collective-permute-start.6 = (bf16[1,3,128,2048]{3,2,1,0:T(8,128)(2,1)S(1)}, bf16[1,3,128,2048]{3,2,1,0:T(8,128)(2,1)S(1)}, u32[]{:S(2)}, u32[]{:S(2)}) collective-permute-start(bf16[1,3,128,2048]{3,2,1,0:T(8,128)(2,1)S(1)} %copy-done.33), channel_id=1, source_target_pairs={{0,20},{4,24},{8,28},{12,0},{16,4},{20,8},{24,12},{28,16},{1,21},{... | collective-permute-start | bytes 4718600 | tf_op jit(solution)/shard_map/ppermute | solution.py:221
  543.2 95.3 %collective-permute-start.7 = (bf16[1,3,128,2048]{3,2,1,0:T(8,128)(2,1)S(1)}, bf16[1,3,128,2048]{3,2,1,0:T(8,128)(2,1)S(1)}, u32[]{:S(2)}, u32[]{:S(2)}) collective-permute-start(bf16[1,3,128,2048]{3,2,1,0:T(8,128)(2,1)S(1)} %copy-done.32), channel_id=1, source_target_pairs={{0,24},{4,28},{8,0},{12,4},{16,8},{20,12},{24,16},{28,20},{1,25},{... | collective-permute-start | bytes 4718600 | tf_op jit(solution)/shard_map/ppermute | solution.py:221
  653.7 11.7 %copy-start.42 = (s32[24]{0:T(128)S(1)}, s32[24]{0:T(128)}, u32[]{:S(2)}) copy-start(s32[24]{0:T(128)} %eq.87) | copy-start | bytes 292
  653.7 11.7 %copy-start.43 = (pred[24]{0:T(512)(128)(4,1)S(1)}, pred[24]{0:T(512)(128)(4,1)}, u32[]{:S(2)}) copy-start(pred[24]{0:T(512)(128)(4,1)} %and.119) | copy-start | bytes 76
  (23 other events, 56.1 us)
Sparse Core Ops, SparseCore 0:
  354.5 145.7 reduce-scatter.1
